TPU v7x, 32 devices: a whole 2x2x4 slice. The times are simulated.
32 devices in a mesh: rows: 2 (over core), cols: 16 (over z, y, x).
Axes of the slice: x: 2, y: 2, z: 4, core: 2. Of those that a mesh axis runs over, the one named last changes fastest.
Arguments:
- jacobian: float32 [32768, 16384], P('rows', 'cols'), may hold values from -0.046875 to 0.046875
- targets: float32 [64, 32768], P(None, 'rows'), may hold values from 0 to 1
- anchor: float32 [64, 16384], P(None, 'cols'), may hold values from -6 to 6
- precision: float32 [16384], P('cols'), may hold values from 0.3 to 3
Outputs:
- samples: float32 [64, 16384], P(None, 'cols')
All inputs are finite; a program needn't handle non-finite values.
Results may differ from a plain program's by a relative error of at most 0.0001.
Values sent between devices are 32-bit elements; how exact they have to be, the bound alone decides.
A program may use at most 128 MiB of HBM per device.

v0:
```python
import math

import jax
import jax.numpy as jnp
from jax import lax
from jax.sharding import PartitionSpec as P

STEPS = 3


def body(jacobian, targets, anchor, precision):
    row_dev, col_dev = jacobian.shape
    total_params = col_dev * lax.axis_size("cols")
    clip_level = 0.2 * math.sqrt(row_dev * lax.axis_size("rows") / total_params)
    share_cols = col_dev // lax.axis_size("rows")
    col_offset = lax.axis_index("rows") * share_cols
    anchor_part = lax.dynamic_slice_in_dim(anchor, col_offset, share_cols, 1)
    weight_part = lax.dynamic_slice_in_dim(precision, col_offset, share_cols, 0)
    theta_part = anchor_part
    velocity = jnp.zeros_like(anchor_part)

    def whole_theta(part_now):
        return lax.all_gather(part_now, "rows", axis=1, tiled=True)

    for step in range(STEPS):
        theta_full = anchor if step == 0 else whole_theta(theta_part)
        part_logits = lax.dot_general(
            theta_full,
            jacobian,
            (((1,), (1,)), ((), ())),
            precision=lax.Precision.HIGHEST,
            preferred_element_type=jnp.float32,
        )
        logits = lax.psum(part_logits, "cols")
        residual = jax.nn.sigmoid(logits) - targets
        gradient = lax.psum_scatter(
            jnp.dot(
                residual,
                jacobian,
                precision=lax.Precision.HIGHEST,
                preferred_element_type=jnp.float32,
            ),
            "rows",
            scatter_dimension=1,
            tiled=True,
        )
        gradient = gradient + weight_part[None, :] * (theta_part - anchor_part)
        squares = lax.psum(jnp.sum(gradient * gradient, axis=1), ("rows", "cols"))
        scale = jnp.minimum(1.0, clip_level / jnp.sqrt(squares / total_params + 1e-06))
        velocity = 0.9 * velocity + scale[:, None] * gradient
        theta_part = theta_part - 0.5 * velocity
    return whole_theta(theta_part)


def solution(mesh):
    in_specs = (P("rows", "cols"), P(None, "rows"), P(None, "cols"), P("cols"))
    out_specs = P(None, "cols")
    return jax.shard_map(body, mesh=mesh, in_specs=in_specs, out_specs=out_specs, check_vma=False)
```

profile of v0, /device:TPU:0, one launch (start us, length us, event | category | flops | bytes accessed | tf_op | source)
XLA Modules:
  0.0 1030.5 jit_solution(1847494230769114277)
XLA Ops:
  6.5 70.1 %fusion.24 = f32[64,16384]{1,0:T(8,128)} fusion(f32[64,1024]{1,0:T(8,128)} %param.6, f32[16384,1024]{1,0:T(8,128)} %param.4), kind=kOutput, calls=%fused_computation.37 | convolution fusion | flops 12884901888 | bytes 71565312 | tf_op jit(solution)/shard_map/dot_general | solution.py:27
  76.8 170.9 %all-reduce.4.cloned.1.call-done = f32[64,16384]{1,0:T(8,128)} async-done(((f32[64,16384]{1,0:T(8,128)}), f32[64,16384]{1,0:T(8,128)}) %all-reduce.4.cloned.1.call-update) | async-done | bytes 4194320 | tf_op jit(solution)/shard_map/psum | solution.py:34
  247.7 48.5 %fusion.12 = f32[64,1024]{1,0:T(8,128)} fusion(f32[16384,1024]{1,0:T(8,128)} %param.4, f32[64,16384]{1,0:T(8,128)} %param.5, f32[64,16384]{1,0:T(8,128)} %all-reduce.4.cloned.1.call-done), kind=kOutput, calls=%fused_computation.12 | convolution fusion | flops 12889096192 | bytes 75759616 | tf_op jit(solution)/shard_map/dot_general | solution.py:37
  296.4 6.6 reduce-scatter.4.cloned.1.call-done
  303.0 1.0 multiply_reduce_fusion.2
  304.0 40.6 %psum.43 = f32[64]{0:T(128)S(1)} all-reduce(f32[64]{0:T(128)S(1)} %get-tuple-element.7), channel_id=1, replica_groups=mesh['rows'=2,'cols'=16] {'rows','cols'}, use_global_device_ids=true, to_apply=%region_3.0 | all-reduce | flops 64 | bytes 512 | tf_op jit(solution)/shard_map/psum | solution.py:48
  344.7 2.0 all_gather.9
  346.7 70.5 %fusion.25 = f32[64,16384]{1,0:T(8,128)} fusion(f32[64,1024]{1,0:T(8,128)S(1)} %all_gather.9, f32[16384,1024]{1,0:T(8,128)} %param.4), kind=kOutput, calls=%fused_computation.38 | convolution fusion | flops 12884901888 | bytes 71565312 | tf_op jit(solution)/shard_map/dot_general | solution.py:27
  417.3 168.1 %all-reduce.6.cloned.1.call-done = f32[64,16384]{1,0:T(8,128)} async-done(((f32[64,16384]{1,0:T(8,128)}), f32[64,16384]{1,0:T(8,128)}) %all-reduce.6.cloned.1.call-update) | async-done | bytes 4194320 | tf_op jit(solution)/shard_map/psum | solution.py:34
  585.5 48.5 %fusion.6 = f32[64,1024]{1,0:T(8,128)} fusion(f32[16384,1024]{1,0:T(8,128)} %param.4, f32[64,16384]{1,0:T(8,128)} %param.5, f32[64,16384]{1,0:T(8,128)} %all-reduce.6.cloned.1.call-done), kind=kOutput, calls=%fused_computation.6 | convolution fusion | flops 12889096192 | bytes 75759616 | tf_op jit(solution)/shard_map/dot_general | solution.py:37
  634.0 6.7 reduce-scatter.6.cloned.1.call-done
  640.7 1.0 multiply_reduce_fusion.1
  641.8 40.5 %psum.45 = f32[64]{0:T(128)S(1)} all-reduce(f32[64]{0:T(128)S(1)} %get-tuple-element.5), channel_id=1, replica_groups=mesh['rows'=2,'cols'=16] {'rows','cols'}, use_global_device_ids=true, to_apply=%region_7.0 | all-reduce | flops 64 | bytes 512 | tf_op jit(solution)/shard_map/psum | solution.py:48
  682.3 0.1 multiply_subtract_fusion.1
  682.4 2.0 all_gather.10
  684.4 70.1 %fusion.26 = f32[64,16384]{1,0:T(8,128)} fusion(f32[64,1024]{1,0:T(8,128)S(1)} %all_gather.10, f32[16384,1024]{1,0:T(8,128)} %param.4), kind=kOutput, calls=%fused_computation.39 | convolution fusion | flops 12884901888 | bytes 71565312 | tf_op jit(solution)/shard_map/dot_general | solution.py:27
  754.6 168.2 %all-reduce.8.cloned.1.call-done = f32[64,16384]{1,0:T(8,128)} async-done(((f32[64,16384]{1,0:T(8,128)}), f32[64,16384]{1,0:T(8,128)}) %all-reduce.8.cloned.1.call-update) | async-done | bytes 4194320 | tf_op jit(solution)/shard_map/psum | solution.py:34
  922.7 48.5 %fusion = f32[64,1024]{1,0:T(8,128)} fusion(f32[16384,1024]{1,0:T(8,128)} %param.4, f32[64,16384]{1,0:T(8,128)} %param.5, f32[64,16384]{1,0:T(8,128)} %all-reduce.8.cloned.1.call-done), kind=kOutput, calls=%fused_computation | convolution fusion | flops 12889096192 | bytes 75759616 | tf_op jit(solution)/shard_map/dot_general | solution.py:37
  971.3 6.8 reduce-scatter.8.cloned.1.call-done
  978.0 1.0 multiply_reduce_fusion
  979.0 40.5 %psum.47 = f32[64]{0:T(128)S(1)} all-reduce(f32[64]{0:T(128)S(1)} %multiply_reduce_fusion), channel_id=1, replica_groups=mesh['rows'=2,'cols'=16] {'rows','cols'}, use_global_device_ids=true, to_apply=%region_11.0 | all-reduce | flops 64 | bytes 512 | tf_op jit(solution)/shard_map/psum | solution.py:48
  1019.5 1.0 multiply_subtract_fusion
  1020.6 2.0 all_gather.11
  1022.6 0.7 copy.9
  (21 shorter events, 0.5 us)
Async XLA Ops:
  6.5 241.2 %all-reduce.4.cloned.1.call-start = ((), (), s32[]{:S(2)}) async-start(), calls=%async_computation.3 | async-start | bytes 8388608 | tf_op jit(solution)/shard_map/psum | solution.py:34
  76.7 219.6 %copy-start.1 = (f32[1024]{0:T(1024)S(1)}, f32[1024]{0:T(1024)}, u32[]{:S(2)}) copy-start(f32[1024]{0:T(1024)} %param.7) | copy-start | bytes 12292
  76.7 226.3 %copy-start = (f32[64,1024]{1,0:T(8,128)S(1)}, f32[64,1024]{1,0:T(8,128)}, u32[]{:S(2)}) copy-start(f32[64,1024]{1,0:T(8,128)} %param.6) | copy-start | bytes 786436
  76.7 226.3 %reduce-scatter.4.cloned.1.call-start = ((), (), s32[]{:S(2)}) async-start(), calls=%async_computation.4 | async-start | bytes 393216 | tf_op jit(solution)/shard_map/reduce_scatter | solution.py:36
  296.2 289.2 %all-reduce.6.cloned.1.call-start = ((), (), s32[]{:S(2)}) async-start(), calls=%async_computation.5 | async-start | bytes 8388608 | tf_op jit(solution)/shard_map/psum | solution.py:34
  417.3 223.5 %reduce-scatter.6.cloned.1.call-start = ((), (), s32[]{:S(2)}) async-start(), calls=%async_computation.6 | async-start | bytes 393216 | tf_op jit(solution)/shard_map/reduce_scatter | solution.py:36
  634.0 288.8 %all-reduce.8.cloned.1.call-start = ((), (), s32[]{:S(2)}) async-start(), calls=%async_computation.7 | async-start | bytes 8388608 | tf_op jit(solution)/shard_map/psum | solution.py:34
  754.5 223.5 %reduce-scatter.8.cloned.1.call-start = ((), (), s32[]{:S(2)}) async-start(), calls=%async_computation.8 | async-start | bytes 393216 | tf_op jit(solution)/shard_map/reduce_scatter | solution.py:36
Sparse Core Ops, SparseCore 0:
  76.8 170.8 all-reduce.3
  296.4 6.5 reduce-scatter.3
  417.4 168.0 all-reduce.5
  634.1 6.5 reduce-scatter.5
  754.6 168.0 all-reduce.7
  971.4 6.5 reduce-scatter.7
where the time goes:
time: 1040 us; the launch traced here: 1030 us
  waiting for transfers between devices  527 us (51%)
  matrix products  356 us (34%)
  blocking collectives  128 us (12%)
  between operations  13.9 us (1%)
    psum x3, waiting for transfers between devices, body(): logits = lax.psum(part_logits, 'cols')  507 us
    dot_general x3, matrix products, body(): lax.dot_general(theta_full, jacobian, (((1,), (1,)), ((), ())), precision...  211 us
    dot_general x3, matrix products, body(): jnp.dot(residual, jacobian, precision=lax.Precision.HIGHEST, preferred_el...  145 us
    psum x3, blocking collectives, body(): squares = lax.psum(jnp.sum(gradient * gradient, axis=1), ('rows', 'cols'))  122 us
  transfers between devices with their start and end apart: 6, of which 6 were waited for; matrix products, arithmetic and copies ran while one was open for 0% of the time, Pallas kernels for 0%

commit v1 on v0

v1 whole, which is shorter than its diff:
```python
import math

import jax
import jax.numpy as jnp
from jax import lax
from jax.sharding import PartitionSpec as P

STEPS = 3
CHUNKS = 4


def swap(value, rows, cols, partner_of):
    pairs = []
    for row in range(rows):
        for col in range(cols):
            to_row, to_col = partner_of(row, col)
            pairs.append((row * cols + col, to_row * cols + to_col))
    return lax.ppermute(value, ("rows", "cols"), pairs)


def body(jacobian, targets, anchor, precision):
    rows, cols = lax.axis_size("rows"), lax.axis_size("cols")
    row_dev, col_dev = jacobian.shape
    total_params = col_dev * cols
    clip_level = 0.2 * math.sqrt(row_dev * rows / total_params)
    bits = cols.bit_length() - 1
    row_bits = rows.bit_length() - 1
    row_at, col_at = lax.axis_index("rows"), lax.axis_index("cols")
    lead = max(1, bits // 4)
    orders = []
    for row in range(rows):
        first = list(range(bits))
        if row % 2:
            first = first[lead : 2 * lead] + first[:lead] + first[2 * lead :]
        orders.append(first)

    def mine(stage):
        bit = jnp.asarray([order[stage] for order in orders], jnp.int32)[row_at]
        return (col_at >> bit) & 1

    def cross(value, stage):
        return swap(value, rows, cols, lambda r, c: (r, c ^ (1 << orders[r][stage])))

    width = row_dev // CHUNKS
    sides = [mine(stage) for stage in range(bits)]

    def reduce_scatter(block):
        for stage in range(bits):
            half = block.shape[1] // 2
            kept = lax.dynamic_slice_in_dim(block, sides[stage] * half, half, 1)
            sent = lax.dynamic_slice_in_dim(block, (1 - sides[stage]) * half, half, 1)
            block = kept + cross(sent, stage)
        return block

    def all_gather(block):
        for stage in reversed(range(bits)):
            other = cross(block, stage)
            low = jnp.where(sides[stage] == 0, block, other)
            high = jnp.where(sides[stage] == 0, other, block)
            block = jnp.concatenate([low, high], axis=1)
        return block

    share = width >> bits
    within = 0
    for stage in range(bits):
        within = within + sides[stage] * (width >> (stage + 1))
    targets_own = [
        lax.dynamic_slice_in_dim(targets, index * width + within, share, 1)
        for index in range(CHUNKS)
    ]
    blocks = [jacobian[index * width : (index + 1) * width] for index in range(CHUNKS)]

    theta = anchor
    velocity = jnp.zeros_like(anchor)
    for step in range(STEPS):
        gradient = precision[None, :] * (theta - anchor)
        residuals = []
        for index in range(CHUNKS):
            part_logits = lax.dot_general(
                theta,
                blocks[index],
                (((1,), (1,)), ((), ())),
                precision=lax.Precision.HIGH,
                preferred_element_type=jnp.float32,
            )
            logits = reduce_scatter(part_logits)
            residuals.append(all_gather(jax.nn.sigmoid(logits) - targets_own[index]))
        total = 0.0
        for index in range(CHUNKS):
            total = total + jnp.dot(
                residuals[index],
                blocks[index],
                precision=lax.Precision.HIGH,
                preferred_element_type=jnp.float32,
            )
        for bit in range(row_bits):
            total = total + swap(total, rows, cols, lambda r, c: (r ^ (1 << bit), c))
        gradient = total + gradient
        squares = jnp.sum(gradient * gradient, axis=1)[None, :]
        for bit in range(bits):
            squares = squares + swap(squares, rows, cols, lambda r, c: (r, c ^ (1 << bit)))
        scale = jnp.minimum(1.0, clip_level / jnp.sqrt(squares[0] / total_params + 1e-06))
        velocity = 0.9 * velocity + scale[:, None] * gradient
        theta = theta - 0.5 * velocity
    return theta


def solution(mesh):
    in_specs = (P("rows", "cols"), P(None, "rows"), P(None, "cols"), P("cols"))
    out_specs = P(None, "cols")
    return jax.shard_map(body, mesh=mesh, in_specs=in_specs, out_specs=out_specs, check_vma=False)
```

time: 1040 us -> 591 us (0.57)
  waiting for transfers between devices: 527 us -> 191 us
  blocking collectives: 128 us -> 0 us
  starting transfers between devices: 0.21 us -> 125 us
  matrix products: 356 us -> 246 us
  between operations: 13.9 us -> 2.72 us
    psum x3 -> x0, waiting for transfers between devices: 507 us -> none  [body(): logits = lax.psum(part_logits, 'cols')]
    ppermute x0 -> x111, waiting for transfers between devices: none -> 191 us  [swap(): return lax.ppermute(value, ('rows', 'cols'), pairs)]
    ppermute x0 -> x111, starting transfers between devices: none -> 125 us  [swap(): return lax.ppermute(value, ('rows', 'cols'), pairs)]
    psum x3 -> x0, blocking collectives: 122 us -> none  [body(): squares = lax.psum(jnp.sum(gradient * gradient, axis=1), ('rows', 'cols'))]
    dot_general x6 -> x24, matrix products: 356 us -> 246 us  [the longest x12 139 us: body(): lax.dot_general(theta, blocks[index], (((1,), (1,)), ((), ())), precision...]
    reduce_scatter x3 -> x0, waiting for transfers between devices: 20.1 us -> none  [body(): lax.psum_scatter(jnp.dot(residual, jacobian, precision=lax.Precision.HIGH...]
  transfers between devices with their start and end apart: 6 -> 111, of which waited for: 6 -> 66; matrix products, arithmetic and copies ran while one was open for 0% -> 22% of each run, Pallas kernels for 0% -> 0%
where the time goes in v1:
time: 591 us; the launch traced here: 584 us
  matrix products  246 us (42%)
  waiting for transfers between devices  191 us (32%)
  starting transfers between devices  125 us (21%)
  other arithmetic  13.3 us (2%)
    ppermute x111, waiting for transfers between devices, swap(): return lax.ppermute(value, ('rows', 'cols'), pairs)  191 us
    dot_general x12, matrix products, body(): lax.dot_general(theta, blocks[index], (((1,), (1,)), ((), ())), precision...  139 us
    ppermute x111, starting transfers between devices, swap(): return lax.ppermute(value, ('rows', 'cols'), pairs)  125 us
    dot_general x12, matrix products, body(): jnp.dot(residuals[index], blocks[index], precision=lax.Precision.HIGH, pr...  108 us
  transfers between devices with their start and end apart: 111, of which 66 were waited for; matrix products, arithmetic and copies ran while one was open for 22% of the time, Pallas kernels for 0%

profile of v1, /device:TPU:0, one launch (start us, length us, event | category | flops | bytes accessed | tf_op | source)
XLA Modules:
  0.0 583.6 jit_solution(4574014413252426829)
XLA Ops:
  0.0 13.4 %fusion.46 = f32[64,4096]{1,0:T(8,128)S(1)} fusion(f32[64,1024]{1,0:T(8,128)} %param.10, f32[16384,1024]{1,0:T(8,128)} %param.8), kind=kOutput, calls=%fused_computation.46 | convolution fusion | flops 1610612736 | bytes 18087936 | tf_op jit(solution)/shard_map/dot_general | solution.py:79
  17.2 11.3 %fusion.10 = f32[64,4096]{1,0:T(8,128)S(1)} fusion(f32[64,1024]{1,0:T(8,128)S(1)} %copy-done, f32[16384,1024]{1,0:T(8,128)} %param.8), kind=kOutput, calls=%fused_computation.10 | convolution fusion | flops 1610612736 | bytes 18087936 | tf_op jit(solution)/shard_map/dot_general | solution.py:79
  29.3 11.3 %fusion.22 = f32[64,4096]{1,0:T(8,128)S(1)} fusion(f32[64,1024]{1,0:T(8,128)S(1)} %copy-done, f32[16384,1024]{1,0:T(8,128)} %param.8), kind=kOutput, calls=%fused_computation.22 | convolution fusion | flops 1610612736 | bytes 18087936 | tf_op jit(solution)/shard_map/dot_general | solution.py:79
  43.5 11.7 %fusion.34 = f32[64,4096]{1,0:T(8,128)S(1)} fusion(f32[64,1024]{1,0:T(8,128)S(1)} %copy-done, f32[16384,1024]{1,0:T(8,128)} %param.8), kind=kOutput, calls=%fused_computation.34 | convolution fusion | flops 1610612736 | bytes 18087936 | tf_op jit(solution)/shard_map/dot_general | solution.py:79
  133.2 8.9 %fusion.8 = f32[64,1024]{1,0:T(8,128)S(1)} fusion(f32[16384,1024]{1,0:T(8,128)} %param.8, f32[64,2048]{1,0:T(8,128)S(1)} %get-tuple-element.44, f32[64,2048]{1,0:T(8,128)S(1)} %get-tuple-element.43), kind=kOutput, calls=%fused_computation.8 | convolution fusion | flops 1610874880 | bytes 18087936 | tf_op jit(solution)/shard_map/dot_general | solution.py:90
  151.3 9.1 %fusion.32 = f32[64,1024]{1,0:T(8,128)S(1)} fusion(f32[16384,1024]{1,0:T(8,128)} %param.8, f32[64,2048]{1,0:T(8,128)S(1)} %get-tuple-element.40, f32[64,2048]{1,0:T(8,128)S(1)} %get-tuple-element.39), kind=kOutput, calls=%fused_computation.32 | convolution fusion | flops 1610874880 | bytes 18087936 | tf_op jit(solution)/shard_map/dot_general | solution.py:90
  160.5 8.9 %fusion.72 = f32[64,1024]{1,0:T(8,128)S(1)} fusion(f32[64,1024]{1,0:T(8,128)S(1)} %fusion.8, f32[64,1024]{1,0:T(8,128)S(1)} %fusion.20, f32[64,1024]{1,0:T(8,128)S(1)} %fusion.32, f32[16384,1024]{1,0:T(8,128)} %param.8, f32[64,2048]{1,0:T(8,128)S(1)} %get-tuple-element.38, f32[64,2048]{1,0:T(8,128)S(1)} %get-tuple-element.37), kind=kOutput, calls=%fused_computation.56 | convolution fusion | flops 1611071488 | bytes 18874368 | tf_op jit(solution)/shard_map/dot_general | solution.py:90
  186.4 11.3 %fusion.42 = f32[64,4096]{1,0:T(8,128)S(1)} fusion(f32[64,1024]{1,0:T(8,128)S(1)} %multiply_subtract_fusion.2, f32[16384,1024]{1,0:T(8,128)} %param.8), kind=kOutput, calls=%fused_computation.42 | convolution fusion | flops 1610612736 | bytes 18087936 | tf_op jit(solution)/shard_map/dot_general | solution.py:79
  197.7 11.3 %fusion.6 = f32[64,4096]{1,0:T(8,128)S(1)} fusion(f32[64,1024]{1,0:T(8,128)S(1)} %multiply_subtract_fusion.2, f32[16384,1024]{1,0:T(8,128)} %param.8), kind=kOutput, calls=%fused_computation.6 | convolution fusion | flops 1610612736 | bytes 18087936 | tf_op jit(solution)/shard_map/dot_general | solution.py:79
  209.0 11.5 %fusion.18 = f32[64,4096]{1,0:T(8,128)S(1)} fusion(f32[64,1024]{1,0:T(8,128)S(1)} %multiply_subtract_fusion.2, f32[16384,1024]{1,0:T(8,128)} %param.8), kind=kOutput, calls=%fused_computation.18 | convolution fusion | flops 1610612736 | bytes 18087936 | tf_op jit(solution)/shard_map/dot_general | solution.py:79
  220.6 11.3 %fusion.30 = f32[64,4096]{1,0:T(8,128)S(1)} fusion(f32[64,1024]{1,0:T(8,128)S(1)} %multiply_subtract_fusion.2, f32[16384,1024]{1,0:T(8,128)} %param.8), kind=kOutput, calls=%fused_computation.30 | convolution fusion | flops 1610612736 | bytes 18087936 | tf_op jit(solution)/shard_map/dot_general | solution.py:79
  244.7 9.5 %collective-permute-done.61 = f32[64,2048]{1,0:T(8,128)S(1)} collective-permute-done((f32[64,2048]{1,0:T(8,128)S(1)}, f32[64,2048]{1,0:T(8,128)S(1)}, u32[]{:S(2)}, u32[]{:S(2)}) %collective-permute-start.61) | collective-permute-done | bytes 524320 | tf_op jit(solution)/shard_map/ppermute | solution.py:18
  331.8 9.3 %fusion.4 = f32[64,1024]{1,0:T(8,128)S(1)} fusion(f32[16384,1024]{1,0:T(8,128)} %param.8, f32[64,2048]{1,0:T(8,128)S(1)} %get-tuple-element.36, f32[64,2048]{1,0:T(8,128)S(1)} %get-tuple-element.35), kind=kOutput, calls=%fused_computation.4 | convolution fusion | flops 1610874880 | bytes 18087936 | tf_op jit(solution)/shard_map/dot_general | solution.py:90
  350.3 8.9 %fusion.28 = f32[64,1024]{1,0:T(8,128)S(1)} fusion(f32[16384,1024]{1,0:T(8,128)} %param.8, f32[64,2048]{1,0:T(8,128)S(1)} %get-tuple-element.32, f32[64,2048]{1,0:T(8,128)S(1)} %get-tuple-element.31), kind=kOutput, calls=%fused_computation.28 | convolution fusion | flops 1610874880 | bytes 18087936 | tf_op jit(solution)/shard_map/dot_general | solution.py:90
  359.3 8.9 %fusion.66 = f32[64,1024]{1,0:T(8,128)S(1)} fusion(f32[64,1024]{1,0:T(8,128)S(1)} %fusion.4, f32[64,1024]{1,0:T(8,128)S(1)} %fusion.16, f32[64,1024]{1,0:T(8,128)S(1)} %fusion.28, f32[16384,1024]{1,0:T(8,128)} %param.8, f32[64,2048]{1,0:T(8,128)S(1)} %get-tuple-element.30, f32[64,2048]{1,0:T(8,128)S(1)} %get-tuple-element.29), kind=kOutput, calls=%fused_computation.54 | convolution fusion | flops 1611071488 | bytes 18874368 | tf_op jit(solution)/shard_map/dot_general | solution.py:90
  385.3 11.5 %fusion.38 = f32[64,4096]{1,0:T(8,128)S(1)} fusion(f32[64,1024]{1,0:T(8,128)S(1)} %multiply_subtract_fusion.1, f32[16384,1024]{1,0:T(8,128)} %param.8), kind=kOutput, calls=%fused_computation.38 | convolution fusion | flops 1610612736 | bytes 18087936 | tf_op jit(solution)/shard_map/dot_general | solution.py:79
  396.8 11.3 %fusion.2 = f32[64,4096]{1,0:T(8,128)S(1)} fusion(f32[64,1024]{1,0:T(8,128)S(1)} %multiply_subtract_fusion.1, f32[16384,1024]{1,0:T(8,128)} %param.8), kind=kOutput, calls=%fused_computation.2 | convolution fusion | flops 1610612736 | bytes 18087936 | tf_op jit(solution)/shard_map/dot_general | solution.py:79
  408.1 11.3 %fusion.14 = f32[64,4096]{1,0:T(8,128)S(1)} fusion(f32[64,1024]{1,0:T(8,128)S(1)} %multiply_subtract_fusion.1, f32[16384,1024]{1,0:T(8,128)} %param.8), kind=kOutput, calls=%fused_computation.14 | convolution fusion | flops 1610612736 | bytes 18087936 | tf_op jit(solution)/shard_map/dot_general | solution.py:79
  419.4 11.5 %fusion.26 = f32[64,4096]{1,0:T(8,128)S(1)} fusion(f32[64,1024]{1,0:T(8,128)S(1)} %multiply_subtract_fusion.1, f32[16384,1024]{1,0:T(8,128)} %param.8), kind=kOutput, calls=%fused_computation.26 | convolution fusion | flops 1610612736 | bytes 18087936 | tf_op jit(solution)/shard_map/dot_general | solution.py:79
  442.9 11.0 %collective-permute-done.98 = f32[64,2048]{1,0:T(8,128)S(1)} collective-permute-done((f32[64,2048]{1,0:T(8,128)S(1)}, f32[64,2048]{1,0:T(8,128)S(1)}, u32[]{:S(2)}, u32[]{:S(2)}) %collective-permute-start.98) | collective-permute-done | bytes 524320 | tf_op jit(solution)/shard_map/ppermute | solution.py:18
  529.0 8.9 %fusion = f32[64,1024]{1,0:T(8,128)S(1)} fusion(f32[16384,1024]{1,0:T(8,128)} %param.8, f32[64,2048]{1,0:T(8,128)S(1)} %get-tuple-element.28, f32[64,2048]{1,0:T(8,128)S(1)} %get-tuple-element.27), kind=kOutput, calls=%fused_computation | convolution fusion | flops 1610874880 | bytes 18087936 | tf_op jit(solution)/shard_map/dot_general | solution.py:90
  538.1 9.2 %fusion.12 = f32[64,1024]{1,0:T(8,128)S(1)} fusion(f32[16384,1024]{1,0:T(8,128)} %param.8, f32[64,2048]{1,0:T(8,128)S(1)} %get-tuple-element.26, f32[64,2048]{1,0:T(8,128)S(1)} %get-tuple-element.25), kind=kOutput, calls=%fused_computation.12 | convolution fusion | flops 1610874880 | bytes 18087936 | tf_op jit(solution)/shard_map/dot_general | solution.py:90
  547.3 8.9 %fusion.24 = f32[64,1024]{1,0:T(8,128)S(1)} fusion(f32[16384,1024]{1,0:T(8,128)} %param.8, f32[64,2048]{1,0:T(8,128)S(1)} %get-tuple-element.24, f32[64,2048]{1,0:T(8,128)S(1)} %get-tuple-element.23), kind=kOutput, calls=%fused_computation.24 | convolution fusion | flops 1610874880 | bytes 18087936 | tf_op jit(solution)/shard_map/dot_general | solution.py:90
  556.4 8.9 %fusion.60 = f32[64,1024]{1,0:T(8,128)S(1)} fusion(f32[64,1024]{1,0:T(8,128)S(1)} %fusion, f32[64,1024]{1,0:T(8,128)S(1)} %fusion.12, f32[64,1024]{1,0:T(8,128)S(1)} %fusion.24, f32[16384,1024]{1,0:T(8,128)} %param.8, f32[64,2048]{1,0:T(8,128)S(1)} %get-tuple-element.22, f32[64,2048]{1,0:T(8,128)S(1)} %get-tuple-element.21), kind=kOutput, calls=%fused_computation.52 | convolution fusion | flops 1611071488 | bytes 18874368 | tf_op jit(solution)/shard_map/dot_general | solution.py:90
  (418 shorter events, 331.7 us)
Async XLA Ops:
  14.3 43.0 %collective-permute-start = (f32[64,2048]{1,0:T(8,128)}, f32[64,2048]{1,0:T(8,128)}, u32[]{:S(2)}, u32[]{:S(2)}) collective-permute-start(f32[64,2048]{1,0:T(8,128)} %constant_dynamic-slice_fusion.47), channel_id=1, source_target_pairs={{0,1},{1,0},{2,3},{3,2},{4,5},{5,4},{6,7},{7,6},{8,9},{9,8},{10,11... | collective-permute-start | bytes 1572872 | tf_op jit(solution)/shard_map/ppermute | solution.py:18
  29.3 31.4 %collective-permute-start.24 = (f32[64,2048]{1,0:T(8,128)}, f32[64,2048]{1,0:T(8,128)}, u32[]{:S(2)}, u32[]{:S(2)}) collective-permute-start(f32[64,2048]{1,0:T(8,128)} %constant_dynamic-slice_fusion.33), channel_id=1, source_target_pairs={{0,1},{1,0},{2,3},{3,2},{4,5},{5,4},{6,7},{7,6},{8,9},{9,8},{10,11... | collective-permute-start | bytes 1572872 | tf_op jit(solution)/shard_map/ppermute | solution.py:18
  41.5 20.5 %collective-permute-start.16 = (f32[64,2048]{1,0:T(8,128)}, f32[64,2048]{1,0:T(8,128)}, u32[]{:S(2)}, u32[]{:S(2)}) collective-permute-start(f32[64,2048]{1,0:T(8,128)} %constant_dynamic-slice_fusion.38), channel_id=1, source_target_pairs={{0,1},{1,0},{2,3},{3,2},{4,5},{5,4},{6,7},{7,6},{8,9},{9,8},{10,11... | collective-permute-start | bytes 1572872 | tf_op jit(solution)/shard_map/ppermute | solution.py:18
  121.8 20.3 %collective-permute-start.23 = (f32[64,2048]{1,0:T(8,128)S(1)}, f32[64,2048]{1,0:T(8,128)S(1)}, u32[]{:S(2)}, u32[]{:S(2)}) collective-permute-start(f32[64,2048]{1,0:T(8,128)S(1)} %pad_maximum_fusion.2), channel_id=1, source_target_pairs={{0,1},{1,0},{2,3},{3,2},{4,5},{5,4},{6,7},{7,6},{8,9},{9,8},{10,11... | collective-permute-start | bytes 1572872 | tf_op jit(solution)/shard_map/ppermute | solution.py:18
  127.4 23.8 %collective-permute-start.15 = (f32[64,2048]{1,0:T(8,128)S(1)}, f32[64,2048]{1,0:T(8,128)S(1)}, u32[]{:S(2)}, u32[]{:S(2)}) collective-permute-start(f32[64,2048]{1,0:T(8,128)S(1)} %pad_maximum_fusion.1), channel_id=1, source_target_pairs={{0,1},{1,0},{2,3},{3,2},{4,5},{5,4},{6,7},{7,6},{8,9},{9,8},{10,11... | collective-permute-start | bytes 1572872 | tf_op jit(solution)/shard_map/ppermute | solution.py:18
  133.0 27.3 %collective-permute-start.7 = (f32[64,2048]{1,0:T(8,128)S(1)}, f32[64,2048]{1,0:T(8,128)S(1)}, u32[]{:S(2)}, u32[]{:S(2)}) collective-permute-start(f32[64,2048]{1,0:T(8,128)S(1)} %pad_maximum_fusion), channel_id=1, source_target_pairs={{0,1},{1,0},{2,3},{3,2},{4,5},{5,4},{6,7},{7,6},{8,9},{9,8},{10,11... | collective-permute-start | bytes 1572872 | tf_op jit(solution)/shard_map/ppermute | solution.py:18
  234.0 20.2 %collective-permute-start.61 = (f32[64,2048]{1,0:T(8,128)S(1)}, f32[64,2048]{1,0:T(8,128)S(1)}, u32[]{:S(2)}, u32[]{:S(2)}) collective-permute-start(f32[64,2048]{1,0:T(8,128)S(1)} %constant_dynamic-slice_fusion.17), channel_id=1, source_target_pairs={{0,1},{1,0},{2,3},{3,2},{4,5},{5,4},{6,7},{7,6},{8,9},{9,8},{10,11... | collective-permute-start | bytes 1572872 | tf_op jit(solution)/shard_map/ppermute | solution.py:18
  234.2 28.7 %collective-permute-start.53 = (f32[64,2048]{1,0:T(8,128)S(1)}, f32[64,2048]{1,0:T(8,128)S(1)}, u32[]{:S(2)}, u32[]{:S(2)}) collective-permute-start(f32[64,2048]{1,0:T(8,128)S(1)} %constant_dynamic-slice_fusion.21), channel_id=1, source_target_pairs={{0,1},{1,0},{2,3},{3,2},{4,5},{5,4},{6,7},{7,6},{8,9},{9,8},{10,11... | collective-permute-start | bytes 1572872 | tf_op jit(solution)/shard_map/ppermute | solution.py:18
  236.3 33.0 %collective-permute-start.45 = (f32[64,2048]{1,0:T(8,128)S(1)}, f32[64,2048]{1,0:T(8,128)S(1)}, u32[]{:S(2)}, u32[]{:S(2)}) collective-permute-start(f32[64,2048]{1,0:T(8,128)S(1)} %constant_dynamic-slice_fusion.25), channel_id=1, source_target_pairs={{0,1},{1,0},{2,3},{3,2},{4,5},{5,4},{6,7},{7,6},{8,9},{9,8},{10,11... | collective-permute-start | bytes 1572872 | tf_op jit(solution)/shard_map/ppermute | solution.py:18
  243.3 27.2 %collective-permute-start.38 = (f32[64,1024]{1,0:T(8,128)S(1)}, f32[64,1024]{1,0:T(8,128)S(1)}, u32[]{:S(2)}, u32[]{:S(2)}) collective-permute-start(f32[64,1024]{1,0:T(8,128)S(1)} %constant_dynamic-slice_fusion.28), channel_id=1, source_target_pairs={{0,2},{1,3},{2,0},{3,1},{4,6},{5,7},{6,4},{7,5},{8,10},{9,11},{10,... | collective-permute-start | bytes 786440 | tf_op jit(solution)/shard_map/ppermute | solution.py:18
  307.7 21.9 %collective-permute-start.43 = (f32[64,1024]{1,0:T(8,128)S(1)}, f32[64,1024]{1,0:T(8,128)S(1)}, u32[]{:S(2)}, u32[]{:S(2)}) collective-permute-start(f32[64,1024]{1,0:T(8,128)S(1)} %pad_maximum_fusion.16), channel_id=1, source_target_pairs={{0,2},{1,3},{2,0},{3,1},{4,6},{5,7},{6,4},{7,5},{8,10},{9,11},{10,... | collective-permute-start | bytes 786440 | tf_op jit(solution)/shard_map/ppermute | solution.py:18
  312.9 18.8 %collective-permute-start.68 = (f32[64,2048]{1,0:T(8,128)S(1)}, f32[64,2048]{1,0:T(8,128)S(1)}, u32[]{:S(2)}, u32[]{:S(2)}) collective-permute-start(f32[64,2048]{1,0:T(8,128)S(1)} %pad_maximum_fusion.7), channel_id=1, source_target_pairs={{0,1},{1,0},{2,3},{3,2},{4,5},{5,4},{6,7},{7,6},{8,9},{9,8},{10,11... | collective-permute-start | bytes 1572872 | tf_op jit(solution)/shard_map/ppermute | solution.py:18
  318.5 22.6 %collective-permute-start.60 = (f32[64,2048]{1,0:T(8,128)S(1)}, f32[64,2048]{1,0:T(8,128)S(1)}, u32[]{:S(2)}, u32[]{:S(2)}) collective-permute-start(f32[64,2048]{1,0:T(8,128)S(1)} %pad_maximum_fusion.6), channel_id=1, source_target_pairs={{0,1},{1,0},{2,3},{3,2},{4,5},{5,4},{6,7},{7,6},{8,9},{9,8},{10,11... | collective-permute-start | bytes 1572872 | tf_op jit(solution)/shard_map/ppermute | solution.py:18
  324.1 26.0 %collective-permute-start.52 = (f32[64,2048]{1,0:T(8,128)S(1)}, f32[64,2048]{1,0:T(8,128)S(1)}, u32[]{:S(2)}, u32[]{:S(2)}) collective-permute-start(f32[64,2048]{1,0:T(8,128)S(1)} %pad_maximum_fusion.5), channel_id=1, source_target_pairs={{0,1},{1,0},{2,3},{3,2},{4,5},{5,4},{6,7},{7,6},{8,9},{9,8},{10,11... | collective-permute-start | bytes 1572872 | tf_op jit(solution)/shard_map/ppermute | solution.py:18
  329.8 29.5 %collective-permute-start.44 = (f32[64,2048]{1,0:T(8,128)S(1)}, f32[64,2048]{1,0:T(8,128)S(1)}, u32[]{:S(2)}, u32[]{:S(2)}) collective-permute-start(f32[64,2048]{1,0:T(8,128)S(1)} %pad_maximum_fusion.4), channel_id=1, source_target_pairs={{0,1},{1,0},{2,3},{3,2},{4,5},{5,4},{6,7},{7,6},{8,9},{9,8},{10,11... | collective-permute-start | bytes 1572872 | tf_op jit(solution)/shard_map/ppermute | solution.py:18
  431.2 22.7 %collective-permute-start.98 = (f32[64,2048]{1,0:T(8,128)S(1)}, f32[64,2048]{1,0:T(8,128)S(1)}, u32[]{:S(2)}, u32[]{:S(2)}) collective-permute-start(f32[64,2048]{1,0:T(8,128)S(1)} %constant_dynamic-slice_fusion.1), channel_id=1, source_target_pairs={{0,1},{1,0},{2,3},{3,2},{4,5},{5,4},{6,7},{7,6},{8,9},{9,8},{10,11... | collective-permute-start | bytes 1572872 | tf_op jit(solution)/shard_map/ppermute | solution.py:18
  433.2 29.2 %collective-permute-start.90 = (f32[64,2048]{1,0:T(8,128)S(1)}, f32[64,2048]{1,0:T(8,128)S(1)}, u32[]{:S(2)}, u32[]{:S(2)}) collective-permute-start(f32[64,2048]{1,0:T(8,128)S(1)} %constant_dynamic-slice_fusion.5), channel_id=1, source_target_pairs={{0,1},{1,0},{2,3},{3,2},{4,5},{5,4},{6,7},{7,6},{8,9},{9,8},{10,11... | collective-permute-start | bytes 1572872 | tf_op jit(solution)/shard_map/ppermute | solution.py:18
  433.4 34.9 %collective-permute-start.82 = (f32[64,2048]{1,0:T(8,128)S(1)}, f32[64,2048]{1,0:T(8,128)S(1)}, u32[]{:S(2)}, u32[]{:S(2)}) collective-permute-start(f32[64,2048]{1,0:T(8,128)S(1)} %constant_dynamic-slice_fusion.9), channel_id=1, source_target_pairs={{0,1},{1,0},{2,3},{3,2},{4,5},{5,4},{6,7},{7,6},{8,9},{9,8},{10,11... | collective-permute-start | bytes 1572872 | tf_op jit(solution)/shard_map/ppermute | solution.py:18
  442.8 25.7 %collective-permute-start.75 = (f32[64,1024]{1,0:T(8,128)S(1)}, f32[64,1024]{1,0:T(8,128)S(1)}, u32[]{:S(2)}, u32[]{:S(2)}) collective-permute-start(f32[64,1024]{1,0:T(8,128)S(1)} %constant_dynamic-slice_fusion.12), channel_id=1, source_target_pairs={{0,2},{1,3},{2,0},{3,1},{4,6},{5,7},{6,4},{7,5},{8,10},{9,11},{10,... | collective-permute-start | bytes 786440 | tf_op jit(solution)/shard_map/ppermute | solution.py:18
  505.2 17.7 %collective-permute-start.88 = (f32[64,1024]{1,0:T(8,128)S(1)}, f32[64,1024]{1,0:T(8,128)S(1)}, u32[]{:S(2)}, u32[]{:S(2)}) collective-permute-start(f32[64,1024]{1,0:T(8,128)S(1)} %pad_maximum_fusion.21), channel_id=1, source_target_pairs={{0,2},{1,3},{2,0},{3,1},{4,6},{5,7},{6,4},{7,5},{8,10},{9,11},{10,... | collective-permute-start | bytes 786440 | tf_op jit(solution)/shard_map/ppermute | solution.py:18
  505.9 22.6 %collective-permute-start.80 = (f32[64,1024]{1,0:T(8,128)S(1)}, f32[64,1024]{1,0:T(8,128)S(1)}, u32[]{:S(2)}, u32[]{:S(2)}) collective-permute-start(f32[64,1024]{1,0:T(8,128)S(1)} %pad_maximum_fusion.20), channel_id=1, source_target_pairs={{0,2},{1,3},{2,0},{3,1},{4,6},{5,7},{6,4},{7,5},{8,10},{9,11},{10,... | collective-permute-start | bytes 786440 | tf_op jit(solution)/shard_map/ppermute | solution.py:18
  517.4 20.6 %collective-permute-start.97 = (f32[64,2048]{1,0:T(8,128)S(1)}, f32[64,2048]{1,0:T(8,128)S(1)}, u32[]{:S(2)}, u32[]{:S(2)}) collective-permute-start(f32[64,2048]{1,0:T(8,128)S(1)} %pad_maximum_fusion.10), channel_id=1, source_target_pairs={{0,1},{1,0},{2,3},{3,2},{4,5},{5,4},{6,7},{7,6},{8,9},{9,8},{10,11... | collective-permute-start | bytes 1572872 | tf_op jit(solution)/shard_map/ppermute | solution.py:18
  523.0 24.3 %collective-permute-start.89 = (f32[64,2048]{1,0:T(8,128)S(1)}, f32[64,2048]{1,0:T(8,128)S(1)}, u32[]{:S(2)}, u32[]{:S(2)}) collective-permute-start(f32[64,2048]{1,0:T(8,128)S(1)} %pad_maximum_fusion.9), channel_id=1, source_target_pairs={{0,1},{1,0},{2,3},{3,2},{4,5},{5,4},{6,7},{7,6},{8,9},{9,8},{10,11... | collective-permute-start | bytes 1572872 | tf_op jit(solution)/shard_map/ppermute | solution.py:18
  528.6 27.7 %collective-permute-start.81 = (f32[64,2048]{1,0:T(8,128)S(1)}, f32[64,2048]{1,0:T(8,128)S(1)}, u32[]{:S(2)}, u32[]{:S(2)}) collective-permute-start(f32[64,2048]{1,0:T(8,128)S(1)} %pad_maximum_fusion.8), channel_id=1, source_target_pairs={{0,1},{1,0},{2,3},{3,2},{4,5},{5,4},{6,7},{7,6},{8,9},{9,8},{10,11... | collective-permute-start | bytes 1572872 | tf_op jit(solution)/shard_map/ppermute | solution.py:18
  (91 other events, 787.5 us)

commit v2 on v1

--- a/solution.py
+++ b/solution.py
@@ -3,10 +3,72 @@
 import jax
 import jax.numpy as jnp
 from jax import lax
+from jax.experimental import pallas as pl
+from jax.experimental.pallas import tpu as pltpu
 from jax.sharding import PartitionSpec as P
 
 STEPS = 3
 CHUNKS = 4
+TILE = 512
+VMEM_LIMIT = 40 << 20
+
+
+def split(value):
+    high = value.astype(jnp.bfloat16)
+    low = (value - high.astype(jnp.float32)).astype(jnp.bfloat16)
+    return high, low
+
+
+def logits_kernel(theta_ref, jacobian_ref, out_ref):
+    samples = theta_ref.shape[0]
+    weights = jnp.concatenate(split(theta_ref[...]), axis=0)
+    high, low = split(jacobian_ref[...])
+    contract = (((1,), (1,)), ((), ()))
+    both = lax.dot_general(high, weights, contract, preferred_element_type=jnp.float32)
+    both += lax.dot_general(low, weights, contract, preferred_element_type=jnp.float32)
+    both = both.T
+    out_ref[...] = both[:samples] + both[samples:]
+
+
+def gradient_kernel(residual_ref, jacobian_ref, out_ref):
+    samples = residual_ref.shape[0]
+    left = jnp.concatenate(split(residual_ref[...]), axis=0)
+    high, low = split(jacobian_ref[...])
+    both = jnp.dot(left, high, preferred_element_type=jnp.float32)
+    both += jnp.dot(left, low, preferred_element_type=jnp.float32)
+    term = both[:samples] + both[samples:]
+
+    @pl.when(pl.program_id(0) == 0)
+    def _():
+        out_ref[...] = term
+
+    @pl.when(pl.program_id(0) > 0)
+    def _():
+        out_ref[...] += term
+
+
+def on_rows(kernel, left, jacobian, index, width, reduce):
+    samples, col_dev = left.shape[0], jacobian.shape[1]
+    tile = math.gcd(TILE, width)
+    tiles = width // tile
+    moving = pl.BlockSpec((samples, tile), lambda at: (0, at))
+    fixed = pl.BlockSpec((samples, col_dev), lambda at: (0, 0))
+    return pl.pallas_call(
+        kernel,
+        grid=(tiles,),
+        in_specs=[
+            moving if reduce else fixed,
+            pl.BlockSpec((tile, col_dev), lambda at: (index * tiles + at, 0)),
+        ],
+        out_specs=fixed if reduce else moving,
+        out_shape=jax.ShapeDtypeStruct((samples, col_dev if reduce else width), jnp.float32),
+        compiler_params=pltpu.CompilerParams(vmem_limit_bytes=VMEM_LIMIT),
+        cost_estimate=pl.CostEstimate(
+            flops=16 * samples * width * col_dev,
+            bytes_accessed=4 * width * col_dev,
+            transcendentals=0,
+        ),
+    )(left, jacobian)
 
 
 def swap(value, rows, cols, partner_of):
@@ -68,7 +130,6 @@
         lax.dynamic_slice_in_dim(targets, index * width + within, share, 1)
         for index in range(CHUNKS)
     ]
-    blocks = [jacobian[index * width : (index + 1) * width] for index in range(CHUNKS)]
 
     theta = anchor
     velocity = jnp.zeros_like(anchor)
@@ -76,22 +137,13 @@
         gradient = precision[None, :] * (theta - anchor)
         residuals = []
         for index in range(CHUNKS):
-            part_logits = lax.dot_general(
-                theta,
-                blocks[index],
-                (((1,), (1,)), ((), ())),
-                precision=lax.Precision.HIGH,
-                preferred_element_type=jnp.float32,
-            )
+            part_logits = on_rows(logits_kernel, theta, jacobian, index, width, False)
             logits = reduce_scatter(part_logits)
             residuals.append(all_gather(jax.nn.sigmoid(logits) - targets_own[index]))
         total = 0.0
         for index in range(CHUNKS):
-            total = total + jnp.dot(
-                residuals[index],
-                blocks[index],
-                precision=lax.Precision.HIGH,
-                preferred_element_type=jnp.float32,
+            total = total + on_rows(
+                gradient_kernel, residuals[index], jacobian, index, width, True
             )
         for bit in range(row_bits):
             total = total + swap(total, rows, cols, lambda r, c: (r ^ (1 << bit), c))

time: 591 us -> 578 us (0.978)
  Pallas kernels: 0 us -> 249 us
  matrix products: 246 us -> 0 us
  waiting for transfers between devices: 191 us -> 177 us
    pallas_call x0 -> x24, Pallas kernels: none -> 249 us  [on_rows(): pl.pallas_call(kernel, grid=(tiles,), in_specs=[moving if reduce else fix...]
    dot_general x24 -> x0, matrix products: 246 us -> none  [the longest x12 139 us: body(): lax.dot_general(theta, blocks[index], (((1,), (1,)), ((), ())), precision...]
    ppermute x111, waiting for transfers between devices: 191 us -> 177 us  [swap(): return lax.ppermute(value, ('rows', 'cols'), pairs)]
  transfers between devices with their start and end apart: 111 -> 111, of which waited for: 66 -> 66; matrix products, arithmetic and copies ran while one was open for 22% -> 2% of each run, Pallas kernels for 0% -> 25%
where the time goes in v2:
time: 578 us; the launch traced here: 576 us
  Pallas kernels  249 us (43%)
  waiting for transfers between devices  177 us (31%)
  starting transfers between devices  126 us (22%)
  other arithmetic  14.1 us (2%)
  local copies, waits for them, and re-layouts  6.65 us (1%)
    pallas_call x24, Pallas kernels, on_rows(): pl.pallas_call(kernel, grid=(tiles,), in_specs=[moving if reduce else fix...  249 us
    ppermute x111, waiting for transfers between devices, swap(): return lax.ppermute(value, ('rows', 'cols'), pairs)  177 us
    ppermute x111, starting transfers between devices, swap(): return lax.ppermute(value, ('rows', 'cols'), pairs)  126 us
  transfers between devices with their start and end apart: 111, of which 66 were waited for; matrix products, arithmetic and copies ran while one was open for 2% of the time, Pallas kernels for 25%

profile of v2, /device:TPU:0, one launch (start us, length us, event | category | flops | bytes accessed | tf_op | source)
XLA Modules:
  0.0 575.8 jit_solution(18441609869123116736)
XLA Ops:
  1.0 10.9 %shard_map.82 = f32[64,4096]{1,0:T(8,128)S(1)} custom-call(f32[64,1024]{1,0:T(8,128)S(1)} %copy-done, f32[16384,1024]{1,0:T(8,128)} %jacobian_ref.47), custom_call_target="tpu_custom_call" | custom-call | flops 4294967296 | bytes 16777216 | tf_op jit(solution)/shard_map/pallas_call | solution.py:56
  15.7 10.9 %shard_map.86 = f32[64,4096]{1,0:T(8,128)S(1)} custom-call(f32[64,1024]{1,0:T(8,128)S(1)} %copy-done, f32[16384,1024]{1,0:T(8,128)} %jacobian_ref.47), custom_call_target="tpu_custom_call" | custom-call | flops 4294967296 | bytes 16777216 | tf_op jit(solution)/shard_map/pallas_call | solution.py:56
  27.4 10.9 %shard_map.88 = f32[64,4096]{1,0:T(8,128)S(1)} custom-call(f32[64,1024]{1,0:T(8,128)S(1)} %copy-done, f32[16384,1024]{1,0:T(8,128)} %jacobian_ref.47), custom_call_target="tpu_custom_call" | custom-call | flops 4294967296 | bytes 16777216 | tf_op jit(solution)/shard_map/pallas_call | solution.py:56
  41.2 10.9 %shard_map.84 = f32[64,4096]{1,0:T(8,128)S(1)} custom-call(f32[64,1024]{1,0:T(8,128)S(1)} %copy-done, f32[16384,1024]{1,0:T(8,128)} %jacobian_ref.47), custom_call_target="tpu_custom_call" | custom-call | flops 4294967296 | bytes 16777216 | tf_op jit(solution)/shard_map/pallas_call | solution.py:56
  131.9 9.8 %shard_map.85 = f32[64,1024]{1,0:T(8,128)S(1)} custom-call(f32[64,4096]{1,0:T(8,128)S(1)} %pad_maximum_fusion.1.residual_ref, f32[16384,1024]{1,0:T(8,128)} %jacobian_ref.47), custom_call_target="tpu_custom_call" | custom-call | flops 4294967296 | bytes 16777216 | tf_op jit(solution)/shard_map/pallas_call | solution.py:56
  142.0 9.8 %shard_map.83 = f32[64,1024]{1,0:T(8,128)S(1)} custom-call(f32[64,4096]{1,0:T(8,128)S(1)} %pad_maximum_fusion.residual_ref, f32[16384,1024]{1,0:T(8,128)} %jacobian_ref.47), custom_call_target="tpu_custom_call" | custom-call | flops 4294967296 | bytes 16777216 | tf_op jit(solution)/shard_map/pallas_call | solution.py:56
  151.8 9.8 %shard_map.87 = f32[64,1024]{1,0:T(8,128)S(1)} custom-call(f32[64,4096]{1,0:T(8,128)S(1)} %pad_maximum_fusion.2.residual_ref, f32[16384,1024]{1,0:T(8,128)} %jacobian_ref.47), custom_call_target="tpu_custom_call" | custom-call | flops 4294967296 | bytes 16777216 | tf_op jit(solution)/shard_map/pallas_call | solution.py:56
  161.9 9.9 %shard_map.89 = f32[64,1024]{1,0:T(8,128)S(1)} custom-call(f32[64,4096]{1,0:T(8,128)S(1)} %pad_maximum_fusion.3.residual_ref, f32[16384,1024]{1,0:T(8,128)} %jacobian_ref.47), custom_call_target="tpu_custom_call" | custom-call | flops 4294967296 | bytes 16777216 | tf_op jit(solution)/shard_map/pallas_call | solution.py:56
  191.8 10.9 %shard_map.90 = f32[64,4096]{1,0:T(8,128)S(1)} custom-call(f32[64,1024]{1,0:T(8,128)S(1)} %multiply_subtract_fusion.2.theta_ref, f32[16384,1024]{1,0:T(8,128)} %jacobian_ref.47), custom_call_target="tpu_custom_call" | custom-call | flops 4294967296 | bytes 16777216 | tf_op jit(solution)/shard_map/pallas_call | solution.py:56
  202.7 10.9 %shard_map.94 = f32[64,4096]{1,0:T(8,128)S(1)} custom-call(f32[64,1024]{1,0:T(8,128)S(1)} %multiply_subtract_fusion.2.theta_ref, f32[16384,1024]{1,0:T(8,128)} %jacobian_ref.47), custom_call_target="tpu_custom_call" | custom-call | flops 4294967296 | bytes 16777216 | tf_op jit(solution)/shard_map/pallas_call | solution.py:56
  213.6 11.1 %shard_map.96 = f32[64,4096]{1,0:T(8,128)S(1)} custom-call(f32[64,1024]{1,0:T(8,128)S(1)} %multiply_subtract_fusion.2.theta_ref, f32[16384,1024]{1,0:T(8,128)} %jacobian_ref.47), custom_call_target="tpu_custom_call" | custom-call | flops 4294967296 | bytes 16777216 | tf_op jit(solution)/shard_map/pallas_call | solution.py:56
  227.1 10.9 %shard_map.92 = f32[64,4096]{1,0:T(8,128)S(1)} custom-call(f32[64,1024]{1,0:T(8,128)S(1)} %multiply_subtract_fusion.2.theta_ref, f32[16384,1024]{1,0:T(8,128)} %jacobian_ref.47), custom_call_target="tpu_custom_call" | custom-call | flops 4294967296 | bytes 16777216 | tf_op jit(solution)/shard_map/pallas_call | solution.py:56
  325.0 9.8 %shard_map.93 = f32[64,1024]{1,0:T(8,128)S(1)} custom-call(f32[64,4096]{1,0:T(8,128)S(1)} %pad_maximum_fusion.5.residual_ref, f32[16384,1024]{1,0:T(8,128)} %jacobian_ref.47), custom_call_target="tpu_custom_call" | custom-call | flops 4294967296 | bytes 16777216 | tf_op jit(solution)/shard_map/pallas_call | solution.py:56
  335.1 9.8 %shard_map.91 = f32[64,1024]{1,0:T(8,128)S(1)} custom-call(f32[64,4096]{1,0:T(8,128)S(1)} %pad_maximum_fusion.4.residual_ref, f32[16384,1024]{1,0:T(8,128)} %jacobian_ref.47), custom_call_target="tpu_custom_call" | custom-call | flops 4294967296 | bytes 16777216 | tf_op jit(solution)/shard_map/pallas_call | solution.py:56
  345.0 9.8 %shard_map.95 = f32[64,1024]{1,0:T(8,128)S(1)} custom-call(f32[64,4096]{1,0:T(8,128)S(1)} %pad_maximum_fusion.6.residual_ref, f32[16384,1024]{1,0:T(8,128)} %jacobian_ref.47), custom_call_target="tpu_custom_call" | custom-call | flops 4294967296 | bytes 16777216 | tf_op jit(solution)/shard_map/pallas_call | solution.py:56
  355.1 9.9 %shard_map.97 = f32[64,1024]{1,0:T(8,128)S(1)} custom-call(f32[64,4096]{1,0:T(8,128)S(1)} %pad_maximum_fusion.7.residual_ref, f32[16384,1024]{1,0:T(8,128)} %jacobian_ref.47), custom_call_target="tpu_custom_call" | custom-call | flops 4294967296 | bytes 16777216 | tf_op jit(solution)/shard_map/pallas_call | solution.py:56
  382.1 10.9 %shard_map.98 = f32[64,4096]{1,0:T(8,128)S(1)} custom-call(f32[64,1024]{1,0:T(8,128)S(1)} %multiply_subtract_fusion.1.theta_ref, f32[16384,1024]{1,0:T(8,128)} %jacobian_ref.47), custom_call_target="tpu_custom_call" | custom-call | flops 4294967296 | bytes 16777216 | tf_op jit(solution)/shard_map/pallas_call | solution.py:56
  393.0 10.9 %shard_map.102 = f32[64,4096]{1,0:T(8,128)S(1)} custom-call(f32[64,1024]{1,0:T(8,128)S(1)} %multiply_subtract_fusion.1.theta_ref, f32[16384,1024]{1,0:T(8,128)} %jacobian_ref.47), custom_call_target="tpu_custom_call" | custom-call | flops 4294967296 | bytes 16777216 | tf_op jit(solution)/shard_map/pallas_call | solution.py:56
  403.9 10.9 %shard_map.104 = f32[64,4096]{1,0:T(8,128)S(1)} custom-call(f32[64,1024]{1,0:T(8,128)S(1)} %multiply_subtract_fusion.1.theta_ref, f32[16384,1024]{1,0:T(8,128)} %jacobian_ref.47), custom_call_target="tpu_custom_call" | custom-call | flops 4294967296 | bytes 16777216 | tf_op jit(solution)/shard_map/pallas_call | solution.py:56
  419.2 10.9 %shard_map.100 = f32[64,4096]{1,0:T(8,128)S(1)} custom-call(f32[64,1024]{1,0:T(8,128)S(1)} %multiply_subtract_fusion.1.theta_ref, f32[16384,1024]{1,0:T(8,128)} %jacobian_ref.47), custom_call_target="tpu_custom_call" | custom-call | flops 4294967296 | bytes 16777216 | tf_op jit(solution)/shard_map/pallas_call | solution.py:56
  432.9 10.1 %collective-permute-done.98 = f32[64,2048]{1,0:T(8,128)S(1)} collective-permute-done((f32[64,2048]{1,0:T(8,128)S(1)}, f32[64,2048]{1,0:T(8,128)S(1)}, u32[]{:S(2)}, u32[]{:S(2)}) %collective-permute-start.98) | collective-permute-done | bytes 524320 | tf_op jit(solution)/shard_map/ppermute | solution.py:80
  517.9 9.8 %shard_map.101 = f32[64,1024]{1,0:T(8,128)S(1)} custom-call(f32[64,4096]{1,0:T(8,128)S(1)} %pad_maximum_fusion.9.residual_ref, f32[16384,1024]{1,0:T(8,128)} %jacobian_ref.47), custom_call_target="tpu_custom_call" | custom-call | flops 4294967296 | bytes 16777216 | tf_op jit(solution)/shard_map/pallas_call | solution.py:56
  537.9 9.8 %shard_map.103 = f32[64,1024]{1,0:T(8,128)S(1)} custom-call(f32[64,4096]{1,0:T(8,128)S(1)} %pad_maximum_fusion.10.residual_ref, f32[16384,1024]{1,0:T(8,128)} %jacobian_ref.47), custom_call_target="tpu_custom_call" | custom-call | flops 4294967296 | bytes 16777216 | tf_op jit(solution)/shard_map/pallas_call | solution.py:56
  548.0 9.9 %shard_map.105 = f32[64,1024]{1,0:T(8,128)S(1)} custom-call(f32[64,4096]{1,0:T(8,128)S(1)} %pad_maximum_fusion.11.residual_ref, f32[16384,1024]{1,0:T(8,128)} %jacobian_ref.47), custom_call_target="tpu_custom_call" | custom-call | flops 4294967296 | bytes 16777216 | tf_op jit(solution)/shard_map/pallas_call | solution.py:56
  (463 shorter events, 323.8 us)
Async XLA Ops:
  12.8 41.5 %collective-permute-start = (f32[64,2048]{1,0:T(8,128)}, f32[64,2048]{1,0:T(8,128)}, u32[]{:S(2)}, u32[]{:S(2)}) collective-permute-start(f32[64,2048]{1,0:T(8,128)} %constant_dynamic-slice_fusion.47), channel_id=1, source_target_pairs={{0,1},{1,0},{2,3},{3,2},{4,5},{5,4},{6,7},{7,6},{8,9},{9,8},{10,11... | collective-permute-start | bytes 1572872 | tf_op jit(solution)/shard_map/ppermute | solution.py:80
  27.4 30.2 %collective-permute-start.16 = (f32[64,2048]{1,0:T(8,128)}, f32[64,2048]{1,0:T(8,128)}, u32[]{:S(2)}, u32[]{:S(2)}) collective-permute-start(f32[64,2048]{1,0:T(8,128)} %constant_dynamic-slice_fusion.38), channel_id=1, source_target_pairs={{0,1},{1,0},{2,3},{3,2},{4,5},{5,4},{6,7},{7,6},{8,9},{9,8},{10,11... | collective-permute-start | bytes 1572872 | tf_op jit(solution)/shard_map/ppermute | solution.py:80
  39.2 19.7 %collective-permute-start.24 = (f32[64,2048]{1,0:T(8,128)}, f32[64,2048]{1,0:T(8,128)}, u32[]{:S(2)}, u32[]{:S(2)}) collective-permute-start(f32[64,2048]{1,0:T(8,128)} %constant_dynamic-slice_fusion.33), channel_id=1, source_target_pairs={{0,1},{1,0},{2,3},{3,2},{4,5},{5,4},{6,7},{7,6},{8,9},{9,8},{10,11... | collective-permute-start | bytes 1572872 | tf_op jit(solution)/shard_map/ppermute | solution.py:80
  124.3 17.5 %collective-permute-start.23 = (f32[64,2048]{1,0:T(8,128)S(1)}, f32[64,2048]{1,0:T(8,128)S(1)}, u32[]{:S(2)}, u32[]{:S(2)}) collective-permute-start(f32[64,2048]{1,0:T(8,128)S(1)} %pad_maximum_fusion.14), channel_id=1, source_target_pairs={{0,1},{1,0},{2,3},{3,2},{4,5},{5,4},{6,7},{7,6},{8,9},{9,8},{10,11... | collective-permute-start | bytes 1572872 | tf_op jit(solution)/shard_map/ppermute | solution.py:80
  129.9 31.8 %collective-permute-start.31 = (f32[64,2048]{1,0:T(8,128)S(1)}, f32[64,2048]{1,0:T(8,128)S(1)}, u32[]{:S(2)}, u32[]{:S(2)}) collective-permute-start(f32[64,2048]{1,0:T(8,128)S(1)} %pad_maximum_fusion.15), channel_id=1, source_target_pairs={{0,1},{1,0},{2,3},{3,2},{4,5},{5,4},{6,7},{7,6},{8,9},{9,8},{10,11... | collective-permute-start | bytes 1572872 | tf_op jit(solution)/shard_map/ppermute | solution.py:80
  224.9 16.8 %collective-permute-start.53 = (f32[64,2048]{1,0:T(8,128)S(1)}, f32[64,2048]{1,0:T(8,128)S(1)}, u32[]{:S(2)}, u32[]{:S(2)}) collective-permute-start(f32[64,2048]{1,0:T(8,128)S(1)} %constant_dynamic-slice_fusion.21), channel_id=1, source_target_pairs={{0,1},{1,0},{2,3},{3,2},{4,5},{5,4},{6,7},{7,6},{8,9},{9,8},{10,11... | collective-permute-start | bytes 1572872 | tf_op jit(solution)/shard_map/ppermute | solution.py:80
  227.0 25.9 %collective-permute-start.61 = (f32[64,2048]{1,0:T(8,128)S(1)}, f32[64,2048]{1,0:T(8,128)S(1)}, u32[]{:S(2)}, u32[]{:S(2)}) collective-permute-start(f32[64,2048]{1,0:T(8,128)S(1)} %constant_dynamic-slice_fusion.17), channel_id=1, source_target_pairs={{0,1},{1,0},{2,3},{3,2},{4,5},{5,4},{6,7},{7,6},{8,9},{9,8},{10,11... | collective-permute-start | bytes 1572872 | tf_op jit(solution)/shard_map/ppermute | solution.py:80
  238.1 24.1 %collective-permute-start.45 = (f32[64,2048]{1,0:T(8,128)S(1)}, f32[64,2048]{1,0:T(8,128)S(1)}, u32[]{:S(2)}, u32[]{:S(2)}) collective-permute-start(f32[64,2048]{1,0:T(8,128)S(1)} %constant_dynamic-slice_fusion.25), channel_id=1, source_target_pairs={{0,1},{1,0},{2,3},{3,2},{4,5},{5,4},{6,7},{7,6},{8,9},{9,8},{10,11... | collective-permute-start | bytes 1572872 | tf_op jit(solution)/shard_map/ppermute | solution.py:80
  240.2 23.5 %collective-permute-start.38 = (f32[64,1024]{1,0:T(8,128)S(1)}, f32[64,1024]{1,0:T(8,128)S(1)}, u32[]{:S(2)}, u32[]{:S(2)}) collective-permute-start(f32[64,1024]{1,0:T(8,128)S(1)} %constant_dynamic-slice_fusion.28), channel_id=1, source_target_pairs={{0,2},{1,3},{2,0},{3,1},{4,6},{5,7},{6,4},{7,5},{8,10},{9,11},{10,... | collective-permute-start | bytes 786440 | tf_op jit(solution)/shard_map/ppermute | solution.py:80
  241.8 22.1 %collective-permute-start.54 = (f32[64,1024]{1,0:T(8,128)S(1)}, f32[64,1024]{1,0:T(8,128)S(1)}, u32[]{:S(2)}, u32[]{:S(2)}) collective-permute-start(f32[64,1024]{1,0:T(8,128)S(1)} %constant_dynamic-slice_fusion.20), channel_id=1, source_target_pairs={{0,2},{1,3},{2,0},{3,1},{4,6},{5,7},{6,4},{7,5},{8,10},{9,11},{10,... | collective-permute-start | bytes 786440 | tf_op jit(solution)/shard_map/ppermute | solution.py:80
  301.2 17.7 %collective-permute-start.59 = (f32[64,1024]{1,0:T(8,128)S(1)}, f32[64,1024]{1,0:T(8,128)S(1)}, u32[]{:S(2)}, u32[]{:S(2)}) collective-permute-start(f32[64,1024]{1,0:T(8,128)S(1)} %pad_maximum_fusion.30), channel_id=1, source_target_pairs={{0,2},{1,3},{2,0},{3,1},{4,6},{5,7},{6,4},{7,5},{8,10},{9,11},{10,... | collective-permute-start | bytes 786440 | tf_op jit(solution)/shard_map/ppermute | solution.py:80
  302.6 21.9 %collective-permute-start.67 = (f32[64,1024]{1,0:T(8,128)S(1)}, f32[64,1024]{1,0:T(8,128)S(1)}, u32[]{:S(2)}, u32[]{:S(2)}) collective-permute-start(f32[64,1024]{1,0:T(8,128)S(1)} %pad_maximum_fusion.31), channel_id=1, source_target_pairs={{0,2},{1,3},{2,0},{3,1},{4,6},{5,7},{6,4},{7,5},{8,10},{9,11},{10,... | collective-permute-start | bytes 786440 | tf_op jit(solution)/shard_map/ppermute | solution.py:80
  307.8 16.9 %collective-permute-start.52 = (f32[64,2048]{1,0:T(8,128)S(1)}, f32[64,2048]{1,0:T(8,128)S(1)}, u32[]{:S(2)}, u32[]{:S(2)}) collective-permute-start(f32[64,2048]{1,0:T(8,128)S(1)} %pad_maximum_fusion.17), channel_id=1, source_target_pairs={{0,1},{1,0},{2,3},{3,2},{4,5},{5,4},{6,7},{7,6},{8,9},{9,8},{10,11... | collective-permute-start | bytes 1572872 | tf_op jit(solution)/shard_map/ppermute | solution.py:80
  319.0 15.9 %collective-permute-start.60 = (f32[64,2048]{1,0:T(8,128)S(1)}, f32[64,2048]{1,0:T(8,128)S(1)}, u32[]{:S(2)}, u32[]{:S(2)}) collective-permute-start(f32[64,2048]{1,0:T(8,128)S(1)} %pad_maximum_fusion.18), channel_id=1, source_target_pairs={{0,1},{1,0},{2,3},{3,2},{4,5},{5,4},{6,7},{7,6},{8,9},{9,8},{10,11... | collective-permute-start | bytes 1572872 | tf_op jit(solution)/shard_map/ppermute | solution.py:80
  324.7 30.2 %collective-permute-start.68 = (f32[64,2048]{1,0:T(8,128)S(1)}, f32[64,2048]{1,0:T(8,128)S(1)}, u32[]{:S(2)}, u32[]{:S(2)}) collective-permute-start(f32[64,2048]{1,0:T(8,128)S(1)} %pad_maximum_fusion.19), channel_id=1, source_target_pairs={{0,1},{1,0},{2,3},{3,2},{4,5},{5,4},{6,7},{7,6},{8,9},{9,8},{10,11... | collective-permute-start | bytes 1572872 | tf_op jit(solution)/shard_map/ppermute | solution.py:80
  417.1 25.9 %collective-permute-start.98 = (f32[64,2048]{1,0:T(8,128)S(1)}, f32[64,2048]{1,0:T(8,128)S(1)}, u32[]{:S(2)}, u32[]{:S(2)}) collective-permute-start(f32[64,2048]{1,0:T(8,128)S(1)} %constant_dynamic-slice_fusion.1), channel_id=1, source_target_pairs={{0,1},{1,0},{2,3},{3,2},{4,5},{5,4},{6,7},{7,6},{8,9},{9,8},{10,11... | collective-permute-start | bytes 1572872 | tf_op jit(solution)/shard_map/ppermute | solution.py:80
  430.1 22.1 %collective-permute-start.82 = (f32[64,2048]{1,0:T(8,128)S(1)}, f32[64,2048]{1,0:T(8,128)S(1)}, u32[]{:S(2)}, u32[]{:S(2)}) collective-permute-start(f32[64,2048]{1,0:T(8,128)S(1)} %constant_dynamic-slice_fusion.9), channel_id=1, source_target_pairs={{0,1},{1,0},{2,3},{3,2},{4,5},{5,4},{6,7},{7,6},{8,9},{9,8},{10,11... | collective-permute-start | bytes 1572872 | tf_op jit(solution)/shard_map/ppermute | solution.py:80
  430.5 22.8 %collective-permute-start.75 = (f32[64,1024]{1,0:T(8,128)S(1)}, f32[64,1024]{1,0:T(8,128)S(1)}, u32[]{:S(2)}, u32[]{:S(2)}) collective-permute-start(f32[64,1024]{1,0:T(8,128)S(1)} %constant_dynamic-slice_fusion.12), channel_id=1, source_target_pairs={{0,2},{1,3},{2,0},{3,1},{4,6},{5,7},{6,4},{7,5},{8,10},{9,11},{10,... | collective-permute-start | bytes 786440 | tf_op jit(solution)/shard_map/ppermute | solution.py:80
  431.8 22.2 %collective-permute-start.91 = (f32[64,1024]{1,0:T(8,128)S(1)}, f32[64,1024]{1,0:T(8,128)S(1)}, u32[]{:S(2)}, u32[]{:S(2)}) collective-permute-start(f32[64,1024]{1,0:T(8,128)S(1)} %constant_dynamic-slice_fusion.4), channel_id=1, source_target_pairs={{0,2},{1,3},{2,0},{3,1},{4,6},{5,7},{6,4},{7,5},{8,10},{9,11},{10,... | collective-permute-start | bytes 786440 | tf_op jit(solution)/shard_map/ppermute | solution.py:80
  492.4 17.8 %collective-permute-start.96 = (f32[64,1024]{1,0:T(8,128)S(1)}, f32[64,1024]{1,0:T(8,128)S(1)}, u32[]{:S(2)}, u32[]{:S(2)}) collective-permute-start(f32[64,1024]{1,0:T(8,128)S(1)} %pad_maximum_fusion.34), channel_id=1, source_target_pairs={{0,2},{1,3},{2,0},{3,1},{4,6},{5,7},{6,4},{7,5},{8,10},{9,11},{10,... | collective-permute-start | bytes 786440 | tf_op jit(solution)/shard_map/ppermute | solution.py:80
  493.1 22.7 %collective-permute-start.104 = (f32[64,1024]{1,0:T(8,128)S(1)}, f32[64,1024]{1,0:T(8,128)S(1)}, u32[]{:S(2)}, u32[]{:S(2)}) collective-permute-start(f32[64,1024]{1,0:T(8,128)S(1)} %pad_maximum_fusion.35), channel_id=1, source_target_pairs={{0,2},{1,3},{2,0},{3,1},{4,6},{5,7},{6,4},{7,5},{8,10},{9,11},{10,... | collective-permute-start | bytes 786440 | tf_op jit(solution)/shard_map/ppermute | solution.py:80
  499.0 18.6 %collective-permute-start.89 = (f32[64,2048]{1,0:T(8,128)S(1)}, f32[64,2048]{1,0:T(8,128)S(1)}, u32[]{:S(2)}, u32[]{:S(2)}) collective-permute-start(f32[64,2048]{1,0:T(8,128)S(1)} %pad_maximum_fusion.21), channel_id=1, source_target_pairs={{0,1},{1,0},{2,3},{3,2},{4,5},{5,4},{6,7},{7,6},{8,9},{9,8},{10,11... | collective-permute-start | bytes 1572872 | tf_op jit(solution)/shard_map/ppermute | solution.py:80
  510.2 17.6 %collective-permute-start.97 = (f32[64,2048]{1,0:T(8,128)S(1)}, f32[64,2048]{1,0:T(8,128)S(1)}, u32[]{:S(2)}, u32[]{:S(2)}) collective-permute-start(f32[64,2048]{1,0:T(8,128)S(1)} %pad_maximum_fusion.22), channel_id=1, source_target_pairs={{0,1},{1,0},{2,3},{3,2},{4,5},{5,4},{6,7},{7,6},{8,9},{9,8},{10,11... | collective-permute-start | bytes 1572872 | tf_op jit(solution)/shard_map/ppermute | solution.py:80
  515.9 31.9 %collective-permute-start.105 = (f32[64,2048]{1,0:T(8,128)S(1)}, f32[64,2048]{1,0:T(8,128)S(1)}, u32[]{:S(2)}, u32[]{:S(2)}) collective-permute-start(f32[64,2048]{1,0:T(8,128)S(1)} %pad_maximum_fusion.23), channel_id=1, source_target_pairs={{0,1},{1,0},{2,3},{3,2},{4,5},{5,4},{6,7},{7,6},{8,9},{9,8},{10,11... | collective-permute-start | bytes 1572872 | tf_op jit(solution)/shard_map/ppermute | solution.py:80
  (106 other events, 1033.8 us)
